TPU v7x, 32 devices: a whole 2x2x4 slice. The times are simulated.
32 devices in a mesh: rep: 4 (over y, x), fsdp: 8 (over z, core).
Axes of the slice: x: 2, y: 2, z: 4, core: 2. Of those that a mesh axis runs over, the one named last changes fastest.
Arguments:
- activations: bfloat16 [4, 6144, 6144], P('rep', 'fsdp'), may hold values from -6 to 6
- out_grads: bfloat16 [4, 6144, 512], P('rep', 'fsdp'), may hold values from -0.078125 to 0.078125
- momentum: float32 [4, 6144, 512], P('rep', 'fsdp'), may hold values from -6 to 6
- indices: int32 [4, 96, 8, 128], P('rep', 'fsdp'), may hold values from 0 to 4095, as said below
- counts: int32 [4], P('rep'), may hold values from 64 to 128, as said below
Outputs:
- new_momentum: float32 [4, 6144, 512], P('rep', 'fsdp')
- step_dir: float32 [6144, 512], P('fsdp')
Inputs may be any that keep to these rules, and one draw needn't show every extreme that they name: `indices`: in each replica's list for one tile the 128 entries are distinct; only the first counts[r] slots of replica r are in use, the others hold further distinct positions that are not chosen. `counts`: the same count holds for every tile of one replica; some replica uses all 128 slots.
All inputs are finite; a program needn't handle non-finite values.
Results may differ from a plain program's by a relative error of at most 0.0003.
Values may be sent and summed in bfloat16 or wider, within the bound.
A program may use at most 192 MiB of HBM per device.

v0:
```python
import math

import jax
import jax.numpy as jnp
from jax import lax
from jax.sharding import PartitionSpec as P

CH = 64


def cosine_table(side):
    freq = lax.broadcasted_iota(jnp.int32, (side, side), 0).astype(jnp.float32)
    place = lax.broadcasted_iota(jnp.int32, (side, side), 1).astype(jnp.float32)
    table = jnp.cos(math.pi * (2.0 * place + 1.0) * freq / (2.0 * side)) * math.sqrt(2.0 / side)
    return jnp.where(freq < 0.5, table * math.sqrt(0.5), table)


def forward_tiles(field, table):
    height, breadth = field.shape
    side = table.shape[0]
    blocks = field.reshape(height // side, side, breadth // side, side)
    result = jnp.einsum("ka,iajb,lb->ijkl", table, blocks, table, precision=lax.Precision.HIGHEST)
    return result.reshape(height // side, breadth // side, side * side)


def inverse_tiles(values, table):
    tile_rows, tile_cols, flat_size = values.shape
    side = table.shape[0]
    grid = values.reshape(tile_rows, tile_cols, side, side)
    blocks = jnp.einsum("ka,ijkl,lb->iajb", table, grid, table, precision=lax.Precision.HIGHEST)
    return blocks.reshape(tile_rows * side, tile_cols * side)


def scatter_slots(values, places, flat_size):
    tile_rows, tile_cols, width_slots = values.shape
    tile_count = tile_rows * tile_cols
    tile_ids = jnp.broadcast_to(
        jnp.arange(tile_count, dtype=jnp.int32)[:, None], (tile_count, width_slots)
    )
    dense = jnp.zeros((tile_count, flat_size), jnp.float32)
    dense = dense.at[tile_ids, places.reshape(tile_count, width_slots)].add(
        values.reshape(tile_count, width_slots)
    )
    return dense.reshape(tile_rows, tile_cols, flat_size)


def token_contract(left, right):
    return lax.dot_general(
        left, right, (((0,), (0,)), ((), ())), preferred_element_type=jnp.float32
    )


def body(activations, out_grads, momentum, indices, counts):
    table = cosine_table(CH)
    inputs = activations[0]
    grads = out_grads[0]
    gradient = lax.psum_scatter(
        token_contract(inputs, grads), "fsdp", scatter_dimension=0, tiled=True
    )
    moment = 0.9 * momentum[0] + gradient
    coefficients = forward_tiles(moment, table)
    places = indices[0]
    picked = jnp.take_along_axis(coefficients, places, axis=2)
    live = lax.broadcasted_iota(jnp.int32, places.shape, 2) < counts[0]
    picked = jnp.where(live, picked, jnp.zeros_like(picked))
    flat_size = CH * CH
    sparse = scatter_slots(picked, places, flat_size)
    new_moment = moment - inverse_tiles(sparse, table)
    total = lax.psum(sparse, "rep")
    decoded = inverse_tiles(total, table)
    step_dir = decoded * lax.rsqrt(decoded * decoded + 0.04)
    return (new_moment[None], step_dir)


def solution(mesh):
    placed = (
        P("rep", "fsdp", None),
        P("rep", "fsdp", None),
        P("rep", "fsdp", None),
        P("rep", "fsdp", None, None),
        P("rep"),
    )
    return jax.shard_map(
        body,
        mesh=mesh,
        in_specs=placed,
        out_specs=(P("rep", "fsdp", None), P("fsdp", None)),
        check_vma=False,
    )
```

profile of v0, /device:TPU:8, one launch (start us, length us, event | category | flops | bytes accessed | tf_op | source)
XLA Modules:
  0.0 447.4 jit_solution(13441428003012626088)
XLA Ops:
  7.2 0.0 copy-start
  7.2 0.0 reduce-scatter.2.cloned.1.call-start
  7.2 1.1 copy-done
  8.3 11.8 %fusion = f32[6144,512]{1,0:T(8,128)} fusion(bf16[1,768,6144]{2,1,0:T(8,128)(2,1)} %param.5, bf16[1,768,512]{2,1,0:T(8,128)(2,1)S(1)} %copy-done), kind=kOutput, calls=%fused_computation.2 | convolution fusion | flops 4831838208 | bytes 22806528 | tf_op jit(solution)/shard_map/dot_general | solution.py:48
  20.2 0.0 reduce-scatter.2.cloned.1.call-update
  21.0 0.0 copy-done.7
  21.0 0.1 multiply_reduce_fusion
  21.1 0.1 and_reduce_fusion
  21.3 126.6 %reduce-scatter.2.cloned.1.call-done = f32[768,512]{1,0:T(8,128)} async-done(((f32[6144,512]{1,0:T(8,128)}), f32[768,512]{1,0:T(8,128)}) %reduce-scatter.2.cloned.1.call-update) | async-done | bytes 1572880 | tf_op jit(solution)/shard_map/reduce_scatter | solution.py:57
  147.8 1.8 bitcast_add_fusion
  149.6 0.0 copy-start.3
  149.6 2.2 reshape.103
  151.8 5.4 %fusion.2 = f32[12,8,64,64]{2,3,1,0:T(8,128)S(1)} fusion(f32[12,64,8,64]{3,2,1,0:T(8,128)} %reshape.103, f32[64]{0:T(128)S(1)} %get-tuple-element.3, f32[64]{0:T(128)S(1)} %get-tuple-element.2, pred[64]{0:T(512)(128)(4,1)S(1)} %convert_compare_fusion), kind=kOutput, calls=%fused_computation.4 | convolution fusion | flops 302010368 | bytes 3146304 | tf_op jit(solution)/shard_map/ka,iajb,lb->ijkl/dot_general | solution.py:22
  157.2 4.4 fusion.19
  161.6 2.4 reshape.104
  164.1 94.9 %gather_fusion = f32[12288]{0:T(1024)S(1)} fusion(f32[12,8,4096]{2,1,0:T(8,128)S(1)} %reshape.104, s32[12288]{0:T(1024)S(1)} %fusion.10), kind=kCustom, calls=%fused_computation | custom fusion | bytes 245760 | tf_op jit(solution)/shard_map/jit(take_along_axis)/gather | solution.py:63
  259.0 65.7 %scatter_custom_fusion = f32[393216]{0:T(1024)} fusion(s32[12288]{0:T(1024)S(1)} %select_bitcast_fusion, f32[12288]{0:T(1024)S(1)} %fusion.12, f32[]{:T(128)} %constant.15.clone.1), kind=kCustom, calls=%fused_computation.12 | custom fusion | flops 12288 | bytes 1572868
  324.7 2.4 reshape_reshape.3
  327.1 4.9 %fusion.17 = f32[12,8,64,64]{2,3,1,0:T(8,128)} fusion(f32[12,8,64,64]{3,2,1,0:T(8,128)S(1)} %reshape_reshape.3, f32[64]{0:T(128)S(1)} %get-tuple-element.3, f32[64]{0:T(128)S(1)} %get-tuple-element.2, pred[64]{0:T(512)(128)(4,1)S(1)} %convert_compare_fusion), kind=kOutput, calls=%fused_computation.32 | convolution fusion | flops 302010368 | bytes 3146304 | tf_op jit(solution)/shard_map/ka,ijkl,lb->iajb/dot_general | solution.py:30
  332.0 0.7 all-reduce.2.cloned.1.call-update
  332.8 1.2 copy-done.5
  333.9 2.9 convolution_bitcast_fusion.1
  336.8 3.9 copy.8
  340.7 3.1 reshape.105
  343.8 1.5 subtract_bitcast_fusion
  345.3 79.1 %all-reduce.2.cloned.1.call-done = f32[12,8,64,64]{3,2,1,0:T(8,128)} async-done(((f32[12,8,64,64]{3,2,1,0:T(8,128)}), f32[12,8,64,64]{3,2,1,0:T(8,128)}) %all-reduce.2.cloned.1.call-update) | async-done | bytes 1572880 | tf_op jit(solution)/shard_map/psum | solution.py:69
  424.4 5.1 %fusion.14 = f32[12,8,64,64]{2,3,1,0:T(8,128)S(1)} fusion(f32[12,8,64,64]{3,2,1,0:T(8,128)} %all-reduce.2.cloned.1.call-done, f32[64]{0:T(128)S(1)} %get-tuple-element.3, f32[64]{0:T(128)S(1)} %get-tuple-element.2, pred[64]{0:T(512)(128)(4,1)S(1)} %convert_compare_fusion), kind=kOutput, calls=%fused_computation.29 | convolution fusion | flops 302010368 | bytes 3146304 | tf_op jit(solution)/shard_map/ka,ijkl,lb->iajb/dot_general | solution.py:30
  429.5 2.9 convolution_bitcast_fusion
  432.5 0.0 copy-start.1
  432.5 3.8 copy.9
  436.3 2.8 reshape.108
  439.2 1.4 rsqrt_multiply_fusion
  (23 shorter events, 0.1 us)
Async XLA Ops:
  7.2 1.1 copy-start
  7.2 140.7 %reduce-scatter.2.cloned.1.call-start = ((), (), s32[]{:S(2)}) async-start(), calls=%async_computation.1 | async-start | bytes 14155776 | tf_op jit(solution)/shard_map/reduce_scatter | solution.py:57
  20.1 0.8 copy-start.7
  20.1 0.9 copy-start.8
  20.1 1.0 copy-start.9
  20.1 127.7 %copy-start.6 = (f32[1,768,512]{2,1,0:T(8,128)S(1)}, f32[1,768,512]{2,1,0:T(8,128)}, u32[]{:S(2)}) copy-start(f32[1,768,512]{2,1,0:T(8,128)} %param.7) | copy-start | bytes 4718596
  149.6 7.6 %copy-start.3 = (f32[768,512]{1,0:T(8,128)}, f32[768,512]{1,0:T(8,128)S(1)}, u32[]{:S(2)}) copy-start(f32[768,512]{1,0:T(8,128)S(1)} %bitcast_add_fusion) | copy-start | bytes 4718596
  327.1 4.9 %copy-start.2 = (f32[12,8,64,64]{3,2,1,0:T(8,128)}, f32[12,8,64,64]{3,2,1,0:T(8,128)S(1)}, u32[]{:S(2)}) copy-start(f32[12,8,64,64]{3,2,1,0:T(8,128)S(1)} %reshape_reshape.3) | copy-start | bytes 4718596
  332.0 92.4 %all-reduce.2.cloned.1.call-start = ((), (), s32[]{:S(2)}) async-start(), calls=%async_computation.2 | async-start | bytes 6291456 | tf_op jit(solution)/shard_map/psum | solution.py:69
  332.0 1.9 copy-start.5
  340.7 3.1 copy-start.4
  432.5 8.1 %copy-start.1 = (bf16[1,768,512]{2,1,0:T(8,128)(2,1)S(1)}, bf16[1,768,512]{2,1,0:T(8,128)(2,1)}, u32[]{:S(2)}) copy-start(bf16[1,768,512]{2,1,0:T(8,128)(2,1)} %param.6) | copy-start | bytes 2359300
Sparse Core Ops, SparseCore 0:
  20.3 127.4 reduce-scatter.1
  336.0 88.4 all-reduce.1
where the time goes:
time: 449 us; the launch traced here: 447 us
  waiting for transfers between devices  206 us (46%)
  local copies, waits for them, and re-layouts  118 us (26%)
  other arithmetic  70.5 us (16%)
  matrix products  37.5 us (8%)
  between operations  15 us (3%)
    reduce_scatter x1, waiting for transfers between devices, body(): lax.psum_scatter(token_contract(inputs, grads), 'fsdp', scatter_dimension...  127 us
    gather x1, local copies, waits for them, and re-layouts, body(): picked = jnp.take_along_axis(coefficients, places, axis=2)  94.9 us
    psum x1, waiting for transfers between devices, body(): total = lax.psum(sparse, 'rep')  79.1 us
    unnamed x4, other arithmetic  65.9 us
    dot_general x4, matrix products, inverse_tiles(): jnp.einsum('ka,ijkl,lb->iajb', table, grid, table, precision=lax.Precisio...  15.8 us
    dot_general x1, matrix products, token_contract(): lax.dot_general(left, right, (((0,), (0,)), ((), ())), preferred_element_...  11.8 us
    dot_general x2, matrix products, forward_tiles(): jnp.einsum('ka,iajb,lb->ijkl', table, blocks, table, precision=lax.Precis...  9.82 us
  transfers between devices with their start and end apart: 2, of which 2 were waited for; matrix products, arithmetic and copies ran while one was open for 3% of the time, Pallas kernels for 0%

commit v1 on v0

v1 whole, which is shorter than its diff:
```python
import functools
import math

import jax
import jax.numpy as jnp
import numpy as np
from jax import lax
from jax.experimental import pallas as pl
from jax.experimental.pallas import tpu as pltpu
from jax.sharding import PartitionSpec as P
import ml_dtypes

CH = 64
MESH = pl.DeviceIdType.MESH
LEVELS = 32000.0


def cosine_tables():
    freq = np.arange(CH, dtype=np.float64)[:, None]
    place = np.arange(CH, dtype=np.float64)[None, :]
    table = np.cos(math.pi * (2 * place + 1) * freq / (2 * CH)) * math.sqrt(2.0 / CH)
    table[0] *= math.sqrt(0.5)

    def pieces(matrix):
        whole = matrix.astype(np.float32)
        head = whole.astype(ml_dtypes.bfloat16)
        tail = (whole - head.astype(np.float32)).astype(ml_dtypes.bfloat16)
        return [head, tail]

    left = np.kron(np.eye(2), table)
    right = np.kron(np.eye(4), table)
    return (
        np.stack(pieces(left) + pieces(left.T)),
        np.stack(pieces(right.T) + pieces(right)),
    )


def split(value):
    head = value.astype(jnp.bfloat16)
    return head, (value - head.astype(jnp.float32)).astype(jnp.bfloat16)


def dot(a, b, contract=((1,), (0,))):
    return lax.dot_general(a, b, (contract, ((), ())), preferred_element_type=jnp.float32)


def transform(field, left, right, way):
    lh, ll = left[2 * way], left[2 * way + 1]
    rh, rl = right[2 * way], right[2 * way + 1]
    parts = []
    for start in range(0, field.shape[1], 256):
        fh, fl = split(field[:, start : start + 256])
        parts.append(dot(fh, rh) + (dot(fh, rl) + dot(fl, rh)))
    yh, yl = split(jnp.concatenate(parts, axis=1))
    return dot(lh, yh) + (dot(lh, yl) + dot(ll, yh))


def pair_rows(rows, pair):
    a = rows[2 * pair : 2 * pair + 1, :]
    b = rows[2 * pair + 1 : 2 * pair + 2, :]
    return a, b


def row_codes(rows, pair):
    a, b = pair_rows(rows, pair)
    return jnp.concatenate([a >> 6, b >> 6], axis=1)


def column_hot(rows, pair):
    a, b = pair_rows(rows, pair)
    codes = jnp.concatenate([a & 63, (b & 63) + 64], axis=1)
    spots = lax.broadcasted_iota(jnp.int32, (2 * CH, codes.shape[1]), 0)
    return jnp.where(spots == codes, 1.0, 0.0).astype(jnp.bfloat16)


def kernel(
    sizes,
    counts_ref, act_hbm, grad_hbm, mom_hbm, places_ref, left_ref, right_ref,
    new_ref, step_ref,
    own_act, sib_act, own_grad, sib_grad, mom, acc, coded, scales, in_coded, in_scales,
    lists, values, mask, cols_hot, total,
    act_sem, sib_send, sib_recv, misc_sem, out_send, out_recv, rep_send, rep_recv,
):
    lines, reps, rows, chunk, pieces, width, tokens = sizes
    tile_rows, pairs = rows // CH, width // CH // 2
    f = lax.axis_index("fsdp")
    rep = lax.axis_index("rep")
    z, core = f // 2, f % 2
    sibling = {"fsdp": 2 * z + 1 - core}

    def along(step):
        return {"fsdp": 2 * (z + step) + core}

    barrier = pltpu.get_barrier_semaphore()
    pl.semaphore_signal(barrier, inc=1, device_id=sibling, device_id_type=MESH)

    @pl.when(z > 0)
    def _():
        pl.semaphore_signal(barrier, inc=1, device_id=along(-1), device_id_type=MESH)

    @pl.when(z < lines - 1)
    def _():
        pl.semaphore_signal(barrier, inc=1, device_id=along(1), device_id_type=MESH)

    for o in range(1, reps):
        pl.semaphore_signal(
            barrier, inc=1, device_id={"rep": lax.rem(rep + o, reps)}, device_id_type=MESH
        )

    def source(q, lane):
        start = (2 * (q // pieces) + lane) * rows + (q % pieces) * chunk
        return act_hbm.at[:, pl.ds(pl.multiple_of(start, 128), chunk)]

    def own_copy(q):
        return pltpu.make_async_copy(source(q, core), own_act.at[q], act_sem.at[q])

    def sib_copy(q):
        return pltpu.make_async_remote_copy(
            src_ref=source(q, 1 - core), dst_ref=sib_act.at[q],
            send_sem=sib_send.at[q], recv_sem=sib_recv.at[q],
            device_id=sibling, device_id_type=MESH,
        )

    grad_own = pltpu.make_async_copy(grad_hbm, own_grad, misc_sem.at[0])
    mom_own = pltpu.make_async_copy(mom_hbm, mom, misc_sem.at[1])
    grad_sib = pltpu.make_async_remote_copy(
        src_ref=grad_hbm, dst_ref=sib_grad, send_sem=misc_sem.at[2], recv_sem=misc_sem.at[3],
        device_id=sibling, device_id_type=MESH,
    )
    grad_own.start()
    neighbours = 1 + jnp.where(z > 0, 1, 0) + jnp.where(z < lines - 1, 1, 0) + (reps - 1)
    pl.semaphore_wait(barrier, neighbours)
    grad_sib.start()

    def each(k, right, left):
        far, piece = k // pieces, k % pieces

        @pl.when(lines - 1 - far > z)
        def _():
            right((lines - 1 - far) * pieces + piece)

        @pl.when(far < z)
        def _():
            left(far * pieces + piece)

    steps = (lines - 1) * pieces

    def fetch(q):
        own_copy(q).start()
        sib_copy(q).start()

    def fetch_step(k, carry):
        each(k, fetch, fetch)
        return carry

    lax.fori_loop(0, steps, fetch_step, 0)
    for piece in range(pieces):
        fetch(z * pieces + piece)
    mom_own.start()

    slot = lax.broadcasted_iota(jnp.int32, places_ref.shape, 2)
    lists[rep] = jnp.where(slot < counts_ref[0], places_ref[...], -1)

    def list_copy(o, buffer, kind):
        return pltpu.make_async_remote_copy(
            src_ref=buffer.at[rep], dst_ref=buffer.at[rep],
            send_sem=rep_send.at[kind, o], recv_sem=rep_recv.at[kind, o],
            device_id={"rep": lax.rem(rep + o, reps)}, device_id_type=MESH,
        )

    for o in range(1, reps):
        list_copy(o, lists, 0).start()

    grad_own.wait()
    grad_sib.wait()

    def partial(q):
        own_copy(q).wait()
        sib_copy(q).wait_recv()
        over = ((0,), (0,))
        acc[...] = dot(own_act[q], own_grad[...], over) + dot(sib_act[q], sib_grad[...], over)

    def chunk_copies(q, way, step):
        return [
            pltpu.make_async_remote_copy(
                src_ref=src.at[q], dst_ref=dst.at[way, q],
                send_sem=out_send.at[kind, q], recv_sem=out_recv.at[kind, way, q],
                device_id=along(step), device_id_type=MESH,
            )
            for kind, (src, dst) in enumerate(((coded, in_coded), (scales, in_scales)))
        ]

    def add_arrived(q, way, step):
        for copy in chunk_copies(q, way, step):
            copy.wait_recv()
        acc[...] += in_coded[way, q].astype(jnp.int32).astype(jnp.float32) * in_scales[way, q]

    def pass_on(q, way, step):
        value = acc[...]
        top = jnp.maximum(jnp.max(jnp.abs(value), axis=0, keepdims=True), 1e-30)
        scales[q] = top * (1.0 / LEVELS)
        coded[q] = jnp.round(value * (LEVELS / top)).astype(jnp.int32).astype(jnp.int16)
        for copy in chunk_copies(q, way, step):
            copy.start()

    def right(q):
        partial(q)

        @pl.when(z > 0)
        def _():
            add_arrived(q, 0, 1)

        pass_on(q, 0, 1)

    def left(q):
        partial(q)

        @pl.when(z < lines - 1)
        def _():
            add_arrived(q, 1, -1)

        pass_on(q, 1, -1)

    def line_step(k, carry):
        each(k, right, left)
        return carry

    lax.fori_loop(0, 1, line_step, 0)

    def mask_step(i, carry):
        codes = lists[rep, i]
        for pair in range(pairs):
            row = row_codes(codes, pair)
            spots = lax.broadcasted_iota(jnp.int32, (CH, row.shape[1]), 0)
            hot = jnp.where(spots == row, 1.0, 0.0).astype(jnp.bfloat16)
            cols = column_hot(codes, pair)
            mask[pl.ds(pl.multiple_of(i * CH, CH), CH), 2 * CH * pair : 2 * CH * (pair + 1)] = (
                dot(hot, cols, ((1,), (1,)))
            )
        return carry

    lax.fori_loop(0, tile_rows, mask_step, 0)
    lax.fori_loop(1, steps, line_step, 0)

    for o in range(1, reps):
        list_copy(o, lists, 0).wait()

    def hot_step(n, carry):
        codes = lists[n // tile_rows, n % tile_rows]
        for pair in range(pairs):
            cols_hot[n, pair] = column_hot(codes, pair)
        return carry

    lax.fori_loop(0, reps * tile_rows, hot_step, 0)

    mom_own.wait()
    group = 2 * CH

    for piece in range(pieces):
        q = z * pieces + piece
        partial(q)

        @pl.when(z > 0)
        def _():
            add_arrived(q, 0, 1)

        @pl.when(z < lines - 1)
        def _():
            add_arrived(q, 1, -1)

        for part in range(chunk // group):
            start = piece * chunk + part * group
            here = slice(start, start + group)
            moment = 0.9 * mom[here, :] + acc[part * group : (part + 1) * group, :]
            coefficients = transform(moment, left_ref, right_ref, 0)
            chosen = jnp.where(mask[here, :] > 0.5, coefficients, 0.0)
            new_ref[here, :] = moment - transform(chosen, left_ref, right_ref, 1)
            head, tail = split(coefficients)
            for half in range(2):
                i = start // CH + half
                codes = lists[rep, i]
                picks = []
                for pair in range(pairs):
                    at = (slice(half * CH, (half + 1) * CH), slice(2 * CH * pair, 2 * CH * (pair + 1)))
                    cols = cols_hot[rep * tile_rows + i, pair]
                    found = dot(jnp.concatenate([head[at], tail[at]], axis=0), cols)
                    found = found[:CH] + found[CH:]
                    row = row_codes(codes, pair)
                    spots = lax.broadcasted_iota(jnp.int32, found.shape, 0)
                    pick = jnp.sum(jnp.where(spots == row, found, 0.0), axis=0, keepdims=True)
                    picks += [pick[:, : pick.shape[1] // 2], pick[:, pick.shape[1] // 2 :]]
                values[rep, i] = jnp.concatenate(picks, axis=0)

    for o in range(1, reps):
        list_copy(o, values, 1).start()
    for o in range(1, reps):
        list_copy(o, values, 1).wait()

    def total_step(i, carry):
        for pair in range(pairs):
            result = jnp.zeros((2 * CH, 2 * CH), jnp.float32)
            for r in range(reps):
                row = row_codes(lists[r, i], pair)
                a, b = pair_rows(values[r, i], pair)
                head, tail = split(jnp.concatenate([a, b], axis=1))
                spots = lax.broadcasted_iota(jnp.int32, (CH, row.shape[1]), 0)
                hit = spots == row
                both = jnp.concatenate(
                    [
                        jnp.where(hit, head.astype(jnp.float32), 0.0),
                        jnp.where(hit, tail.astype(jnp.float32), 0.0),
                    ],
                    axis=0,
                ).astype(jnp.bfloat16)
                result += dot(both, cols_hot[r * tile_rows + i, pair], ((1,), (1,)))
            total[pl.ds(pl.multiple_of(i * CH, CH), CH), 2 * CH * pair : 2 * CH * (pair + 1)] = (
                result[:CH] + result[CH:]
            )
        return carry

    lax.fori_loop(0, tile_rows, total_step, 0)
    for start in range(0, rows, group):
        decoded = transform(total[start : start + group, :], left_ref, right_ref, 1)
        step_ref[start : start + group, :] = decoded * lax.rsqrt(decoded * decoded + 0.04)

    def sent(way, step):
        def wait(q):
            for copy in chunk_copies(q, way, step):
                copy.wait_send()
            sib_copy(q).wait_send()

        return wait

    def sent_step(k, carry):
        each(k, sent(0, 1), sent(1, -1))
        return carry

    lax.fori_loop(0, steps, sent_step, 0)
    for piece in range(pieces):
        sib_copy(z * pieces + piece).wait_send()


def body(lines, reps, activations, out_grads, momentum, indices, counts):
    inputs, grads, moment, places = activations[0], out_grads[0], momentum[0], indices[0]
    tokens, model = inputs.shape
    owned, width = moment.shape
    tile_cols, slots = places.shape[1:]
    fill = -owned % (2 * CH)
    rows = owned + fill
    if fill:
        inputs = inputs.reshape(tokens, 2 * lines, owned)
        inputs = jnp.pad(inputs, ((0, 0), (0, 0), (0, fill))).reshape(tokens, 2 * lines * rows)
        moment = jnp.pad(moment, ((0, fill), (0, 0)))
        places = jnp.pad(places, ((0, fill // CH), (0, 0), (0, 0)), constant_values=-1)
    tile_rows = rows // CH
    pieces = 3 if rows % (6 * CH) == 0 else rows // (2 * CH)
    chunk = rows // pieces
    count = lines * pieces
    left, right = cosine_tables()
    sizes = (lines, reps, rows, chunk, pieces, width, tokens)
    vmem = pl.BlockSpec(memory_space=pltpu.VMEM)
    hbm = pl.BlockSpec(memory_space=pl.ANY)
    dma = pltpu.SemaphoreType.DMA
    new_moment, step_dir = pl.pallas_call(
        functools.partial(kernel, sizes),
        out_shape=(
            jax.ShapeDtypeStruct((rows, width), jnp.float32),
            jax.ShapeDtypeStruct((rows, width), jnp.float32),
        ),
        in_specs=[pl.BlockSpec(memory_space=pltpu.SMEM), hbm, hbm, hbm, vmem, vmem, vmem],
        out_specs=(vmem, vmem),
        scratch_shapes=[
            pltpu.VMEM((count, tokens, chunk), jnp.bfloat16),
            pltpu.VMEM((count, tokens, chunk), jnp.bfloat16),
            pltpu.VMEM((tokens, width), jnp.bfloat16),
            pltpu.VMEM((tokens, width), jnp.bfloat16),
            pltpu.VMEM((rows, width), jnp.float32),
            pltpu.VMEM((chunk, width), jnp.float32),
            pltpu.VMEM((count, chunk, width), jnp.int16),
            pltpu.VMEM((count, 1, width), jnp.float32),
            pltpu.VMEM((2, count, chunk, width), jnp.int16),
            pltpu.VMEM((2, count, 1, width), jnp.float32),
            pltpu.VMEM((reps, tile_rows, tile_cols, slots), jnp.int32),
            pltpu.VMEM((reps, tile_rows, tile_cols, slots), jnp.float32),
            pltpu.VMEM((rows, width), jnp.float32),
            pltpu.VMEM((reps * tile_rows, tile_cols // 2, 2 * CH, 2 * slots), jnp.bfloat16),
            pltpu.VMEM((rows, width), jnp.float32),
            dma((count,)),
            dma((count,)),
            dma((count,)),
            dma((4,)),
            dma((2, count)),
            dma((2, 2, count)),
            dma((2, reps)),
            dma((2, reps)),
        ],
        compiler_params=pltpu.CompilerParams(
            collective_id=0, has_side_effects=True, vmem_limit_bytes=60 * 1024 * 1024
        ),
        cost_estimate=pl.CostEstimate(
            flops=2 * tokens * model * width, bytes_accessed=2 * tokens * model, transcendentals=0
        ),
    )(counts, inputs, grads, moment, places, jnp.asarray(left), jnp.asarray(right))
    return (new_moment[None, :owned], step_dir[:owned])


def solution(mesh):
    lines, reps = mesh.shape["fsdp"] // 2, mesh.shape["rep"]
    placed = (
        P("rep", "fsdp", None),
        P("rep", "fsdp", None),
        P("rep", "fsdp", None),
        P("rep", "fsdp", None, None),
        P("rep"),
    )
    return jax.shard_map(
        functools.partial(body, lines, reps),
        mesh=mesh,
        in_specs=placed,
        out_specs=(P("rep", "fsdp", None), P("fsdp", None)),
        check_vma=False,
    )
```

time: 449 us -> 101 us (0.22)
  waiting for transfers between devices: 206 us -> 0 us
  local copies, waits for them, and re-layouts: 118 us -> 3.93 us
  Pallas kernels: 0 us -> 95.4 us
  other arithmetic: 70.5 us -> 0 us
  matrix products: 37.5 us -> 0 us
  between operations: 15 us -> 1.29 us
    reduce_scatter x1 -> x0, waiting for transfers between devices: 127 us -> none  [body(): lax.psum_scatter(token_contract(inputs, grads), 'fsdp', scatter_dimension...]
    pallas_call x0 -> x1, Pallas kernels: none -> 95.4 us  [body(): pl.pallas_call(functools.partial(kernel, sizes), out_shape=(jax.ShapeDtyp...]
    gather x1 -> x0, local copies, waits for them, and re-layouts: 94.9 us -> none  [body(): picked = jnp.take_along_axis(coefficients, places, axis=2)]
    psum x1 -> x0, waiting for transfers between devices: 79.1 us -> none  [body(): total = lax.psum(sparse, 'rep')]
    unnamed x4 -> x0, other arithmetic: 65.9 us -> none
    dot_general x7 -> x0, matrix products: 37.5 us -> none  [the longest x4 15.8 us: inverse_tiles(): jnp.einsum('ka,ijkl,lb->iajb', table, grid, table, precision=lax.Precisio...]
    reshape x4 -> x0, local copies, waits for them, and re-layouts: 10.5 us -> none  [the longest x2 5.9 us: inverse_tiles(): return blocks.reshape(tile_rows * side, tile_cols * side)]
    transpose x2 -> x0, local copies, waits for them, and re-layouts: 7.72 us -> none  [inverse_tiles(): jnp.einsum('ka,ijkl,lb->iajb', table, grid, table, precision=lax.Precisio...]
  transfers between devices with their start and end apart: 2 -> 0, of which waited for: 2 -> 0; matrix products, arithmetic and copies ran while one was open for 3% -> 0% of each run, Pallas kernels for 0% -> 0%
where the time goes in v1:
time: 101 us
  Pallas kernels  95.4 us (94%)
  local copies, waits for them, and re-layouts  3.93 us (4%)
  between operations  1.29 us (1%)
    pallas_call x1, Pallas kernels, body(): pl.pallas_call(functools.partial(kernel, sizes), out_shape=(jax.ShapeDtyp...  95.4 us
    unnamed x4, local copies, waits for them, and re-layouts  3.93 us

profile of v1, /device:TPU:8, one launch (start us, length us, event | category | flops | bytes accessed | tf_op | source)
XLA Modules:
  0.0 100.7 jit_solution(13728276264953611253)
XLA Ops:
  1.3 95.4 %shard_map.86 = (f32[768,512]{1,0:T(8,128)}, f32[768,512]{1,0:T(8,128)}) custom-call(s32[1]{0:T(128)S(6)} %copy.11.counts_ref, bf16[768,6144]{1,0:T(8,128)(2,1)} %bitcast.6, bf16[768,512]{1,0:T(8,128)(2,1)} %bitcast.8, f32[768,512]{1,0:T(8,128)} %bitcast.7, s32[12,8,128]{2,1,0:T(8,128)} %bitcast.9, bf16[4,128,128]{2,1,0:T(8,128)(2,1)} %constant.4.clone.left_ref, ...), custom_call_target="tpu_custom_call" | custom-call | flops 4831838208 | bytes 9437184 | tf_op jit(solution)/shard_map/pallas_call | solution.py:364
  96.7 0.0 copy-start
  96.7 2.8 %copy.12 = f32[1,768,512]{2,1,0:T(8,128)} copy(f32[1,768,512]{2,1,0:T(8,128)} %bitcast.5) | data formatting | bytes 3145728
  99.5 0.0 copy-done
  99.5 1.1 %copy.13 = f32[768,512]{1,0:T(8,128)} copy(f32[768,512]{1,0:T(8,128)S(1)} %copy-done) | data formatting | bytes 3145728
Async XLA Ops:
  96.7 2.8 %copy-start = (f32[768,512]{1,0:T(8,128)S(1)}, f32[768,512]{1,0:T(8,128)}, u32[]{:S(2)}) copy-start(f32[768,512]{1,0:T(8,128)} %get-tuple-element.9) | copy-start | bytes 4718596

commit v2 on v1

v2 whole, which is shorter than its diff:
```python
import functools
import math

import jax
import jax.numpy as jnp
import numpy as np
from jax import lax
from jax.experimental import pallas as pl
from jax.experimental.pallas import tpu as pltpu
from jax.sharding import PartitionSpec as P
import ml_dtypes

CH = 64
MESH = pl.DeviceIdType.MESH
LEVELS = 32000.0


def cosine_tables():
    freq = np.arange(CH, dtype=np.float64)[:, None]
    place = np.arange(CH, dtype=np.float64)[None, :]
    table = np.cos(math.pi * (2 * place + 1) * freq / (2 * CH)) * math.sqrt(2.0 / CH)
    table[0] *= math.sqrt(0.5)
    whole = np.kron(np.eye(4), table).astype(np.float32)
    head = whole.astype(ml_dtypes.bfloat16)
    tail = (whole - head.astype(np.float32)).astype(ml_dtypes.bfloat16)
    return np.stack([head.T, tail.T, head, tail])


def split(value):
    head = value.astype(jnp.bfloat16)
    return head, (value - head.astype(jnp.float32)).astype(jnp.bfloat16)


def dot(a, b, contract=((1,), (0,))):
    return lax.dot_general(a, b, (contract, ((), ())), preferred_element_type=jnp.float32)


def transform(field, tables, way):
    height, width = field.shape
    rh, rl = tables[2 * way], tables[2 * way + 1]
    other = 2 - 2 * way
    lh, ll = tables[other, :height, :height], tables[other + 1, :height, :height]
    stack = jnp.concatenate([lh, ll], axis=0)
    parts = []
    for start in range(0, width, 256):
        fh, fl = split(field[:, start : start + 256])
        both = dot(jnp.concatenate([fh, fl], axis=0), rh)
        yh, yl = split(both[:height] + (dot(fh, rl) + both[height:]))
        both = dot(stack, yh)
        parts.append(both[:height] + (dot(lh, yl) + both[height:]))
    return jnp.concatenate(parts, axis=1)


def pair_rows(rows, pair):
    a = rows[2 * pair : 2 * pair + 1, :]
    b = rows[2 * pair + 1 : 2 * pair + 2, :]
    return a, b


def row_codes(rows, pair):
    a, b = pair_rows(rows, pair)
    return jnp.concatenate([a >> 6, b >> 6], axis=1)


def column_hot(rows, pair):
    a, b = pair_rows(rows, pair)
    codes = jnp.concatenate([a & 63, (b & 63) + 64], axis=1)
    spots = lax.broadcasted_iota(jnp.int32, (2 * CH, codes.shape[1]), 0)
    return jnp.where(spots == codes, 1.0, 0.0).astype(jnp.bfloat16)


def kernel(
    sizes,
    counts_ref, act_hbm, grad_hbm, mom_hbm, places_ref, tables,
    new_hbm, dec_hbm,
    own_act, sib_act, own_grad, sib_grad, flipped, mom, acc, coded, scales, in_coded, in_scales,
    lists, values, mask, cols_hot, total, decoded,
    act_sem, sib_send, sib_recv, misc_sem, out_send, out_recv, rep_send, rep_recv, res_sem,
):
    lines, reps, rows, chunk, pieces, width, tokens = sizes
    pairs = width // CH // 2
    tile_rows = rows // CH
    piece_tiles = chunk // CH
    f = lax.axis_index("fsdp")
    rep = lax.axis_index("rep")
    z, core = f // 2, f % 2
    sibling = {"fsdp": 2 * z + 1 - core}

    def along(step):
        return {"fsdp": 2 * (z + step) + core}

    grad_own = pltpu.make_async_copy(grad_hbm, own_grad, misc_sem.at[0])
    mom_own = pltpu.make_async_copy(mom_hbm, mom, misc_sem.at[1])
    grad_own.start()

    barrier = pltpu.get_barrier_semaphore()
    pl.semaphore_signal(barrier, inc=1, device_id=sibling, device_id_type=MESH)

    @pl.when(z > 0)
    def _():
        pl.semaphore_signal(barrier, inc=1, device_id=along(-1), device_id_type=MESH)

    @pl.when(z < lines - 1)
    def _():
        pl.semaphore_signal(barrier, inc=1, device_id=along(1), device_id_type=MESH)

    for o in range(1, reps):
        pl.semaphore_signal(
            barrier, inc=1, device_id={"rep": lax.rem(rep + o, reps)}, device_id_type=MESH
        )

    used = lax.broadcasted_iota(jnp.int32, places_ref.shape[1:], 1) < counts_ref[...]
    for i in range(tile_rows):
        lists[rep, i] = jnp.where(used, places_ref[i], -1)

    def source(q, lane):
        start = (2 * (q // pieces) + lane) * rows + (q % pieces) * chunk
        return act_hbm.at[:, pl.ds(pl.multiple_of(start, 128), chunk)]

    def own_copy(q):
        return pltpu.make_async_copy(source(q, core), own_act.at[q], act_sem.at[q])

    def sib_copy(q):
        return pltpu.make_async_remote_copy(
            src_ref=source(q, 1 - core), dst_ref=sib_act.at[q],
            send_sem=sib_send.at[q], recv_sem=sib_recv.at[q],
            device_id=sibling, device_id_type=MESH,
        )

    grad_sib = pltpu.make_async_remote_copy(
        src_ref=grad_hbm, dst_ref=sib_grad, send_sem=misc_sem.at[2], recv_sem=misc_sem.at[3],
        device_id=sibling, device_id_type=MESH,
    )

    steps = (lines - 1) * pieces
    plain = (lines - 3) * pieces

    def owner(k):
        later = k - plain
        block = jnp.where(later < 0, lines - 1 - k // pieces, 2 - later % 2)
        piece = jnp.where(later < 0, k % pieces, later // 2)
        return block, piece

    def each(k, right, left):
        block, piece = owner(k)

        @pl.when(block > z)
        def _():
            right(block * pieces + piece)

        @pl.when(lines - 1 - block < z)
        def _():
            left((lines - 1 - block) * pieces + piece)

    def fetch(q):
        own_copy(q).start()
        sib_copy(q).start()

    neighbours = 1 + jnp.where(z > 0, 1, 0) + jnp.where(z < lines - 1, 1, 0) + (reps - 1)
    pl.semaphore_wait(barrier, neighbours)
    grad_sib.start()
    each(0, fetch, fetch)

    def list_copy(o):
        return pltpu.make_async_remote_copy(
            src_ref=lists.at[rep], dst_ref=lists.at[rep],
            send_sem=rep_send.at[pieces, o], recv_sem=rep_recv.at[pieces, o],
            device_id={"rep": lax.rem(rep + o, reps)}, device_id_type=MESH,
        )

    def value_copy(o, m):
        part = values.at[rep, pl.ds(m * piece_tiles, piece_tiles)]
        return pltpu.make_async_remote_copy(
            src_ref=part, dst_ref=part,
            send_sem=rep_send.at[m, o], recv_sem=rep_recv.at[m, o],
            device_id={"rep": lax.rem(rep + o, reps)}, device_id_type=MESH,
        )

    grad_own.wait()
    flipped[0] = own_grad[...].T
    grad_sib.wait()
    flipped[1] = sib_grad[...].T
    for k in range(1, min(2, steps)):
        each(k, fetch, fetch)
    for o in range(1, reps):
        list_copy(o).start()

    def partial(q):
        own_copy(q).wait()
        sib_copy(q).wait_recv()
        acc[...] = dot(flipped[0], own_act[q]) + dot(flipped[1], sib_act[q])

    def chunk_copies(q, way, step):
        return [
            pltpu.make_async_remote_copy(
                src_ref=src.at[q], dst_ref=dst.at[way, q],
                send_sem=out_send.at[kind, q], recv_sem=out_recv.at[kind, way, q],
                device_id=along(step), device_id_type=MESH,
            )
            for kind, (src, dst) in enumerate(((coded, in_coded), (scales, in_scales)))
        ]

    def add_arrived(q, way, step):
        for copy in chunk_copies(q, way, step):
            copy.wait_recv()
        acc[...] += in_coded[way, q].astype(jnp.int32).astype(jnp.float32) * in_scales[way, q]

    def pass_on(q, way, step):
        value = acc[...]
        top = jnp.maximum(jnp.max(jnp.abs(value), axis=0, keepdims=True), 1e-30)
        scales[q] = top * (1.0 / LEVELS)
        coded[q] = jnp.round(value * (LEVELS / top)).astype(jnp.int32).astype(jnp.int16)
        for copy in chunk_copies(q, way, step):
            copy.start()

    def right(q):
        partial(q)

        @pl.when(z > 0)
        def _():
            add_arrived(q, 0, 1)

        pass_on(q, 0, 1)

    def left(q):
        partial(q)

        @pl.when(z < lines - 1)
        def _():
            add_arrived(q, 1, -1)

        pass_on(q, 1, -1)

    def sent(way, step):
        def wait(q):
            for copy in chunk_copies(q, way, step):
                copy.wait_send()

        return wait

    def line_step(k, carry):
        @pl.when(k >= 2)
        def _():
            each(k - 2, sent(0, 1), sent(1, -1))

        @pl.when(k + 2 < steps)
        def _():
            each(k + 2, fetch, fetch)

        @pl.when(k < pieces)
        def _():
            fetch(z * pieces + k)

        each(k, right, left)
        return carry

    def mask_step(i, carry):
        codes = lists[rep, i]
        for pair in range(pairs):
            row = row_codes(codes, pair)
            spots = lax.broadcasted_iota(jnp.int32, (CH, row.shape[1]), 0)
            hot = jnp.where(spots == row, 1.0, 0.0).astype(jnp.bfloat16)
            cols = column_hot(codes, pair)
            mask[pl.ds(pl.multiple_of(i * CH, CH), CH), 2 * CH * pair : 2 * CH * (pair + 1)] = (
                dot(hot, cols, ((1,), (1,)))
            )
        return carry

    def hot_step(n, carry):
        codes = lists[n // tile_rows, n % tile_rows]
        for pair in range(pairs):
            cols_hot[n, pair] = column_hot(codes, pair)
        return carry

    def prepare():
        mom_own.start()
        lax.fori_loop(0, tile_rows, mask_step, 0)
        for o in range(1, reps):
            list_copy(o).wait()
        lax.fori_loop(0, reps * tile_rows, hot_step, 0)
        mom_own.wait()

    middle = (z > 0) & (z < lines - 1)

    @pl.when(middle)
    def _():
        prepare()

    line_step(0, 0)

    @pl.when(jnp.logical_not(middle))
    def _():
        prepare()

    lax.fori_loop(1, max(plain, 1), line_step, 0)

    def decode(m):
        for o in range(1, reps):
            value_copy(o, m).wait()

        def tile_step(h, carry):
            i = m * piece_tiles + h
            for pair in range(pairs):
                result = jnp.zeros((2 * CH, 2 * CH), jnp.float32)
                for r in range(reps):
                    row = row_codes(lists[r, i], pair)
                    a, b = pair_rows(values[r, i], pair)
                    head, tail = split(jnp.concatenate([a, b], axis=1))
                    spots = lax.broadcasted_iota(jnp.int32, (CH, row.shape[1]), 0)
                    hit = spots == row
                    both = jnp.concatenate(
                        [
                            jnp.where(hit, head.astype(jnp.float32), 0.0),
                            jnp.where(hit, tail.astype(jnp.float32), 0.0),
                        ],
                        axis=0,
                    ).astype(jnp.bfloat16)
                    result += dot(both, cols_hot[r * tile_rows + i, pair], ((1,), (1,)))
                total[pl.ds(pl.multiple_of(h * CH, CH), CH), 2 * CH * pair : 2 * CH * (pair + 1)] = (
                    result[:CH] + result[CH:]
                )
            return carry

        lax.fori_loop(0, piece_tiles, tile_step, 0)
        decoded[here(m), :] = transform(total[...], tables, 1)
        result_copy(1, m).start()

    def here(m):
        return pl.ds(pl.multiple_of(m * chunk, chunk), chunk)

    def result_copy(kind, m):
        src, dst = ((mom, new_hbm), (decoded, dec_hbm))[kind]
        return pltpu.make_async_copy(src.at[here(m)], dst.at[here(m)], res_sem.at[kind, m])

    def own(m):
        q = z * pieces + m
        partial(q)

        @pl.when(z > 0)
        def _():
            add_arrived(q, 0, 1)

        @pl.when(z < lines - 1)
        def _():
            add_arrived(q, 1, -1)

        moment = 0.9 * mom[here(m), :] + acc[...].T
        coefficients = transform(moment, tables, 0)
        head, tail = split(coefficients)
        for h in range(piece_tiles):
            i = m * piece_tiles + h
            codes = lists[rep, i]
            picks = []
            for pair in range(pairs):
                at = (slice(h * CH, (h + 1) * CH), slice(2 * CH * pair, 2 * CH * (pair + 1)))
                cols = cols_hot[rep * tile_rows + i, pair]
                found = dot(jnp.concatenate([head[at], tail[at]], axis=0), cols)
                found = found[:CH] + found[CH:]
                row = row_codes(codes, pair)
                spots = lax.broadcasted_iota(jnp.int32, found.shape, 0)
                pick = jnp.sum(jnp.where(spots == row, found, 0.0), axis=0, keepdims=True)
                picks += [pick[:, : pick.shape[1] // 2], pick[:, pick.shape[1] // 2 :]]
            values[rep, i] = jnp.concatenate(picks, axis=0)
        for o in range(1, reps):
            value_copy(o, m).start()
        chosen = jnp.where(mask[here(m), :] > 0.5, coefficients, 0.0)
        mom[here(m), :] = moment - transform(chosen, tables, 1)
        result_copy(0, m).start()

    def late_step(m, carry):
        for k in (plain + 2 * m, plain + 2 * m + 1):
            line_step(k, 0)
        own(m)

        @pl.when(m > 0)
        def _():
            decode(m - 1)

        return carry

    lax.fori_loop(0, pieces, late_step, 0)
    decode(pieces - 1)

    for m in range(pieces):
        sib_copy(z * pieces + m).wait_send()
        for kind in range(2):
            result_copy(kind, m).wait()

    def left_step(k, carry):
        def wait(q):
            sib_copy(q).wait_send()

        each(k, wait, wait)
        return carry

    lax.fori_loop(0, steps, left_step, 0)
    for k in range(max(steps - 2, 0), steps):
        each(k, sent(0, 1), sent(1, -1))


def body(lines, reps, activations, out_grads, momentum, indices, counts):
    inputs, grads, moment, places = activations[0], out_grads[0], momentum[0], indices[0]
    tokens, model = inputs.shape
    owned, width = moment.shape
    tile_cols, slots = places.shape[1:]
    chunk = 4 * CH
    fill = -owned % chunk
    rows = owned + fill
    if fill:
        inputs = inputs.reshape(tokens, 2 * lines, owned)
        inputs = jnp.pad(inputs, ((0, 0), (0, 0), (0, fill))).reshape(tokens, 2 * lines * rows)
        moment = jnp.pad(moment, ((0, fill), (0, 0)))
        places = jnp.pad(places, ((0, fill // CH), (0, 0), (0, 0)), constant_values=-1)
    tile_rows = rows // CH
    pieces = rows // chunk
    count = lines * pieces
    sizes = (lines, reps, rows, chunk, pieces, width, tokens)
    vmem = pl.BlockSpec(memory_space=pltpu.VMEM)
    hbm = pl.BlockSpec(memory_space=pl.ANY)
    dma = pltpu.SemaphoreType.DMA
    new_moment, decoded = pl.pallas_call(
        functools.partial(kernel, sizes),
        out_shape=(
            jax.ShapeDtypeStruct((rows, width), jnp.float32),
            jax.ShapeDtypeStruct((rows, width), jnp.float32),
        ),
        in_specs=[vmem, hbm, hbm, hbm, vmem, vmem],
        out_specs=(hbm, hbm),
        scratch_shapes=[
            pltpu.VMEM((count, tokens, chunk), jnp.bfloat16),
            pltpu.VMEM((count, tokens, chunk), jnp.bfloat16),
            pltpu.VMEM((tokens, width), jnp.bfloat16),
            pltpu.VMEM((tokens, width), jnp.bfloat16),
            pltpu.VMEM((2, width, tokens), jnp.bfloat16),
            pltpu.VMEM((rows, width), jnp.float32),
            pltpu.VMEM((width, chunk), jnp.float32),
            pltpu.VMEM((count, width, chunk), jnp.int16),
            pltpu.VMEM((count, 1, chunk), jnp.float32),
            pltpu.VMEM((2, count, width, chunk), jnp.int16),
            pltpu.VMEM((2, count, 1, chunk), jnp.float32),
            pltpu.VMEM((reps, tile_rows, tile_cols, slots), jnp.int32),
            pltpu.VMEM((reps, tile_rows, tile_cols, slots), jnp.float32),
            pltpu.VMEM((rows, width), jnp.float32),
            pltpu.VMEM((reps * tile_rows, tile_cols // 2, 2 * CH, 2 * slots), jnp.bfloat16),
            pltpu.VMEM((chunk, width), jnp.float32),
            pltpu.VMEM((rows, width), jnp.float32),
            dma((count,)),
            dma((count,)),
            dma((count,)),
            dma((4,)),
            dma((2, count)),
            dma((2, 2, count)),
            dma((pieces + 1, reps)),
            dma((pieces + 1, reps)),
            dma((2, pieces)),
        ],
        compiler_params=pltpu.CompilerParams(
            collective_id=0, has_side_effects=True, vmem_limit_bytes=60 * 1024 * 1024
        ),
        cost_estimate=pl.CostEstimate(
            flops=2 * tokens * model * width, bytes_accessed=2 * tokens * model, transcendentals=0
        ),
    )(counts.reshape(1, 1), inputs, grads, moment, places, jnp.asarray(cosine_tables()))
    decoded = decoded[:owned]
    step_dir = decoded * lax.rsqrt(decoded * decoded + 0.04)
    return (new_moment[None, :owned], step_dir)


def solution(mesh):
    lines, reps = mesh.shape["fsdp"] // 2, mesh.shape["rep"]
    placed = (
        P("rep", "fsdp", None),
        P("rep", "fsdp", None),
        P("rep", "fsdp", None),
        P("rep", "fsdp", None, None),
        P("rep"),
    )
    return jax.shard_map(
        functools.partial(body, lines, reps),
        mesh=mesh,
        in_specs=placed,
        out_specs=(P("rep", "fsdp", None), P("fsdp", None)),
        check_vma=False,
    )
```

time: 101 us -> 102 us (level)
  the two profiles are of different devices: /device:TPU:8 before, /device:TPU:16 now
where the time goes in v2:
time: 102 us
  Pallas kernels  96.2 us (94%)
  other arithmetic  2.88 us (3%)
  between operations  1.29 us (1%)
  local copies, waits for them, and re-layouts  1.15 us (1%)
    pallas_call x1, Pallas kernels, body(): pl.pallas_call(functools.partial(kernel, sizes), out_shape=(jax.ShapeDtyp...  96.2 us
    mul x1, other arithmetic, body(): step_dir = decoded * lax.rsqrt(decoded * decoded + 0.04)  2.88 us

profile of v2, /device:TPU:16, one launch (start us, length us, event | category | flops | bytes accessed | tf_op | source)
XLA Modules:
  0.0 101.5 jit_solution(9926468868086578812)
XLA Ops:
  1.3 96.2 %shard_map.77 = (f32[768,512]{1,0:T(8,128)}, f32[768,512]{1,0:T(8,128)}) custom-call(s32[1,1]{1,0:T(1,128)} %bitcast.6.counts_ref, bf16[768,6144]{1,0:T(8,128)(2,1)} %bitcast.8, bf16[768,512]{1,0:T(8,128)(2,1)} %bitcast.10, f32[768,512]{1,0:T(8,128)} %bitcast.9, s32[12,8,128]{2,1,0:T(8,128)} %bitcast.11, bf16[4,256,256]{2,1,0:T(8,128)(2,1)} %constant.4.clone.tables), custom_call_target="tpu_custom_call" | custom-call | flops 4831838208 | bytes 9437184 | tf_op jit(solution)/shard_map/pallas_call | solution.py:421
  97.5 0.0 copy-start
  97.5 2.9 %rsqrt_multiply_fusion = f32[768,512]{1,0:T(8,128)} fusion(f32[768,512]{1,0:T(8,128)} %get-tuple-element.5), kind=kLoop, calls=%fused_computation | loop fusion | flops 1179648 | bytes 3145728 | tf_op jit(solution)/shard_map/mul | solution.py:465
  100.4 0.0 copy-done
  100.4 1.1 %copy.10 = f32[1,768,512]{2,1,0:T(8,128)} copy(f32[1,768,512]{2,1,0:T(8,128)S(1)} %bitcast.7) | data formatting | bytes 3145728
Async XLA Ops:
  97.5 2.9 %copy-start = (f32[768,512]{1,0:T(8,128)S(1)}, f32[768,512]{1,0:T(8,128)}, u32[]{:S(2)}) copy-start(f32[768,512]{1,0:T(8,128)} %get-tuple-element.4) | copy-start | bytes 4718596

commit v3 on v2

--- a/solution.py
+++ b/solution.py
@@ -72,9 +72,9 @@
 def kernel(
     sizes,
     counts_ref, act_hbm, grad_hbm, mom_hbm, places_ref, tables,
-    new_hbm, dec_hbm,
+    new_hbm, step_hbm,
     own_act, sib_act, own_grad, sib_grad, flipped, mom, acc, coded, scales, in_coded, in_scales,
-    lists, values, mask, cols_hot, total, decoded,
+    lists, values, mask, cols_hot, total, directions,
     act_sem, sib_send, sib_recv, misc_sem, out_send, out_recv, rep_send, rep_recv, res_sem,
 ):
     lines, reps, rows, chunk, pieces, width, tokens = sizes
@@ -141,16 +141,20 @@
         piece = jnp.where(later < 0, k % pieces, later // 2)
         return block, piece
 
-    def each(k, right, left):
+    def each(tick, right, left):
+        k = tick - z
         block, piece = owner(k)
 
-        @pl.when(block > z)
+        @pl.when((k >= 0) & (k < steps) & (block > z))
         def _():
             right(block * pieces + piece)
 
-        @pl.when(lines - 1 - block < z)
-        def _():
-            left((lines - 1 - block) * pieces + piece)
+        j = tick - (lines - 1 - z)
+        facing, part = owner(j)
+
+        @pl.when((j >= 0) & (j < steps) & (lines - 1 - facing < z))
+        def _():
+            left((lines - 1 - facing) * pieces + part)
 
     def fetch(q):
         own_copy(q).start()
@@ -180,8 +184,7 @@
     flipped[0] = own_grad[...].T
     grad_sib.wait()
     flipped[1] = sib_grad[...].T
-    for k in range(1, min(2, steps)):
-        each(k, fetch, fetch)
+    each(1, fetch, fetch)
     for o in range(1, reps):
         list_copy(o).start()
 
@@ -243,9 +246,7 @@
         def _():
             each(k - 2, sent(0, 1), sent(1, -1))
 
-        @pl.when(k + 2 < steps)
-        def _():
-            each(k + 2, fetch, fetch)
+        each(k + 2, fetch, fetch)
 
         @pl.when(k < pieces)
         def _():
@@ -292,7 +293,7 @@
     def _():
         prepare()
 
-    lax.fori_loop(1, max(plain, 1), line_step, 0)
+    lax.fori_loop(1, plain + 1, line_step, 0)
 
     def decode(m):
         for o in range(1, reps):
@@ -322,14 +323,15 @@
             return carry
 
         lax.fori_loop(0, piece_tiles, tile_step, 0)
-        decoded[here(m), :] = transform(total[...], tables, 1)
+        result = transform(total[...], tables, 1)
+        directions[here(m), :] = result * lax.rsqrt(result * result + 0.04)
         result_copy(1, m).start()
 
     def here(m):
         return pl.ds(pl.multiple_of(m * chunk, chunk), chunk)
 
     def result_copy(kind, m):
-        src, dst = ((mom, new_hbm), (decoded, dec_hbm))[kind]
+        src, dst = ((mom, new_hbm), (directions, step_hbm))[kind]
         return pltpu.make_async_copy(src.at[here(m)], dst.at[here(m)], res_sem.at[kind, m])
 
     def own(m):
@@ -368,7 +370,7 @@
         result_copy(0, m).start()
 
     def late_step(m, carry):
-        for k in (plain + 2 * m, plain + 2 * m + 1):
+        for k in (plain + 2 * m + 1, plain + 2 * m + 2):
             line_step(k, 0)
         own(m)
 
@@ -393,8 +395,8 @@
         each(k, wait, wait)
         return carry
 
-    lax.fori_loop(0, steps, left_step, 0)
-    for k in range(max(steps - 2, 0), steps):
+    lax.fori_loop(0, steps + 1, left_step, 0)
+    for k in (steps - 1, steps):
         each(k, sent(0, 1), sent(1, -1))
 
 
@@ -418,7 +420,7 @@
     vmem = pl.BlockSpec(memory_space=pltpu.VMEM)
     hbm = pl.BlockSpec(memory_space=pl.ANY)
     dma = pltpu.SemaphoreType.DMA
-    new_moment, decoded = pl.pallas_call(
+    new_moment, step_dir = pl.pallas_call(
         functools.partial(kernel, sizes),
         out_shape=(
             jax.ShapeDtypeStruct((rows, width), jnp.float32),
@@ -461,9 +463,7 @@
             flops=2 * tokens * model * width, bytes_accessed=2 * tokens * model, transcendentals=0
         ),
     )(counts.reshape(1, 1), inputs, grads, moment, places, jnp.asarray(cosine_tables()))
-    decoded = decoded[:owned]
-    step_dir = decoded * lax.rsqrt(decoded * decoded + 0.04)
-    return (new_moment[None, :owned], step_dir)
+    return (new_moment[None, :owned], step_dir[:owned])
 
 
 def solution(mesh):

time: 102 us -> 81.3 us (0.80)
  the two profiles are of different devices: /device:TPU:16 before, /device:TPU:8 now
where the time goes in v3:
time: 81.3 us; the launch traced here: 80.5 us
  Pallas kernels  75.3 us (93%)
  local copies, waits for them, and re-layouts  3.93 us (5%)
  between operations  1.29 us (2%)
    pallas_call x1, Pallas kernels, body(): pl.pallas_call(functools.partial(kernel, sizes), out_shape=(jax.ShapeDtyp...  75.3 us
    unnamed x4, local copies, waits for them, and re-layouts  3.93 us

profile of v3, /device:TPU:8, one launch (start us, length us, event | category | flops | bytes accessed | tf_op | source)
XLA Modules:
  0.0 80.5 jit_solution(9804772587135838514)
XLA Ops:
  1.3 75.3 %shard_map.77 = (f32[768,512]{1,0:T(8,128)}, f32[768,512]{1,0:T(8,128)}) custom-call(s32[1,1]{1,0:T(1,128)} %bitcast.6.counts_ref, bf16[768,6144]{1,0:T(8,128)(2,1)} %bitcast.8, bf16[768,512]{1,0:T(8,128)(2,1)} %bitcast.10, f32[768,512]{1,0:T(8,128)} %bitcast.9, s32[12,8,128]{2,1,0:T(8,128)} %bitcast.11, bf16[4,256,256]{2,1,0:T(8,128)(2,1)} %constant.2.clone.tables), custom_call_target="tpu_custom_call" | custom-call | flops 4831838208 | bytes 9437184 | tf_op jit(solution)/shard_map/pallas_call | solution.py:423
  76.6 0.0 copy-start
  76.6 2.8 %copy.11 = f32[1,768,512]{2,1,0:T(8,128)} copy(f32[1,768,512]{2,1,0:T(8,128)} %bitcast.7) | data formatting | bytes 3145728
  79.4 0.0 copy-done
  79.4 1.1 %copy.12 = f32[768,512]{1,0:T(8,128)} copy(f32[768,512]{1,0:T(8,128)S(1)} %copy-done) | data formatting | bytes 3145728
Async XLA Ops:
  76.6 2.8 %copy-start = (f32[768,512]{1,0:T(8,128)S(1)}, f32[768,512]{1,0:T(8,128)}, u32[]{:S(2)}) copy-start(f32[768,512]{1,0:T(8,128)} %get-tuple-element.9) | copy-start | bytes 4718596

commit v4 on v3

--- a/solution.py
+++ b/solution.py
@@ -72,10 +72,10 @@
 def kernel(
     sizes,
     counts_ref, act_hbm, grad_hbm, mom_hbm, places_ref, tables,
-    new_hbm, step_hbm,
-    own_act, sib_act, own_grad, sib_grad, flipped, mom, acc, coded, scales, in_coded, in_scales,
-    lists, values, mask, cols_hot, total, directions,
-    act_sem, sib_send, sib_recv, misc_sem, out_send, out_recv, rep_send, rep_recv, res_sem,
+    mom, directions,
+    own_act, sib_act, own_grad, sib_grad, flipped, acc, coded, scales, in_coded, in_scales,
+    lists, values, mask, cols_hot, total,
+    act_sem, sib_send, sib_recv, misc_sem, out_send, out_recv, rep_send, rep_recv,
 ):
     lines, reps, rows, chunk, pieces, width, tokens = sizes
     pairs = width // CH // 2
@@ -325,14 +325,9 @@
         lax.fori_loop(0, piece_tiles, tile_step, 0)
         result = transform(total[...], tables, 1)
         directions[here(m), :] = result * lax.rsqrt(result * result + 0.04)
-        result_copy(1, m).start()
 
     def here(m):
         return pl.ds(pl.multiple_of(m * chunk, chunk), chunk)
-
-    def result_copy(kind, m):
-        src, dst = ((mom, new_hbm), (directions, step_hbm))[kind]
-        return pltpu.make_async_copy(src.at[here(m)], dst.at[here(m)], res_sem.at[kind, m])
 
     def own(m):
         q = z * pieces + m
@@ -367,17 +362,16 @@
             value_copy(o, m).start()
         chosen = jnp.where(mask[here(m), :] > 0.5, coefficients, 0.0)
         mom[here(m), :] = moment - transform(chosen, tables, 1)
-        result_copy(0, m).start()
 
     def late_step(m, carry):
         for k in (plain + 2 * m + 1, plain + 2 * m + 2):
             line_step(k, 0)
+
+        @pl.when(m > 0)
+        def _():
+            decode(m - 1)
+
         own(m)
-
-        @pl.when(m > 0)
-        def _():
-            decode(m - 1)
-
         return carry
 
     lax.fori_loop(0, pieces, late_step, 0)
@@ -385,8 +379,6 @@
 
     for m in range(pieces):
         sib_copy(z * pieces + m).wait_send()
-        for kind in range(2):
-            result_copy(kind, m).wait()
 
     def left_step(k, carry):
         def wait(q):
@@ -418,23 +410,22 @@
     count = lines * pieces
     sizes = (lines, reps, rows, chunk, pieces, width, tokens)
     vmem = pl.BlockSpec(memory_space=pltpu.VMEM)
-    hbm = pl.BlockSpec(memory_space=pl.ANY)
+    hbm = pl.BlockSpec(memory_space=pltpu.HBM)
     dma = pltpu.SemaphoreType.DMA
     new_moment, step_dir = pl.pallas_call(
         functools.partial(kernel, sizes),
         out_shape=(
-            jax.ShapeDtypeStruct((rows, width), jnp.float32),
-            jax.ShapeDtypeStruct((rows, width), jnp.float32),
+            pltpu.VMEM((rows, width), jnp.float32),
+            pltpu.VMEM((rows, width), jnp.float32),
         ),
         in_specs=[vmem, hbm, hbm, hbm, vmem, vmem],
-        out_specs=(hbm, hbm),
+        out_specs=(vmem, vmem),
         scratch_shapes=[
             pltpu.VMEM((count, tokens, chunk), jnp.bfloat16),
             pltpu.VMEM((count, tokens, chunk), jnp.bfloat16),
             pltpu.VMEM((tokens, width), jnp.bfloat16),
             pltpu.VMEM((tokens, width), jnp.bfloat16),
             pltpu.VMEM((2, width, tokens), jnp.bfloat16),
-            pltpu.VMEM((rows, width), jnp.float32),
             pltpu.VMEM((width, chunk), jnp.float32),
             pltpu.VMEM((count, width, chunk), jnp.int16),
             pltpu.VMEM((count, 1, chunk), jnp.float32),
@@ -445,7 +436,6 @@
             pltpu.VMEM((rows, width), jnp.float32),
             pltpu.VMEM((reps * tile_rows, tile_cols // 2, 2 * CH, 2 * slots), jnp.bfloat16),
             pltpu.VMEM((chunk, width), jnp.float32),
-            pltpu.VMEM((rows, width), jnp.float32),
             dma((count,)),
             dma((count,)),
             dma((count,)),
@@ -454,10 +444,9 @@
             dma((2, 2, count)),
             dma((pieces + 1, reps)),
             dma((pieces + 1, reps)),
-            dma((2, pieces)),
         ],
         compiler_params=pltpu.CompilerParams(
-            collective_id=0, has_side_effects=True, vmem_limit_bytes=60 * 1024 * 1024
+            collective_id=0, has_side_effects=True, vmem_limit_bytes=48 * 1024 * 1024
         ),
         cost_estimate=pl.CostEstimate(
             flops=2 * tokens * model * width, bytes_accessed=2 * tokens * model, transcendentals=0

time: 81.3 us -> 81 us (level)
  local copies, waits for them, and re-layouts: 3.93 us -> 6.66 us
  Pallas kernels: 75.3 us -> 72.8 us
    unnamed x4 -> x10, local copies, waits for them, and re-layouts: 3.93 us -> 6.66 us
    pallas_call x1, Pallas kernels: 75.3 us -> 72.8 us  [body(): pl.pallas_call(functools.partial(kernel, sizes), out_shape=(pltpu.VMEM((r...]
where the time goes in v4:
time: 81 us; the launch traced here: 80.7 us
  Pallas kernels  72.8 us (90%)
  local copies, waits for them, and re-layouts  6.66 us (8%)
  between operations  1.3 us (2%)
    pallas_call x1, Pallas kernels, body(): pl.pallas_call(functools.partial(kernel, sizes), out_shape=(pltpu.VMEM((r...  72.8 us
    unnamed x10, local copies, waits for them, and re-layouts  6.66 us

profile of v4, /device:TPU:8, one launch (start us, length us, event | category | flops | bytes accessed | tf_op | source)
XLA Modules:
  0.0 80.7 jit_solution(16323434482564566230)
XLA Ops:
  1.3 0.0 copy-start
  1.3 1.4 %copy-done = f32[1,768,512]{2,1,0:T(8,128)S(1)} copy-done((f32[1,768,512]{2,1,0:T(8,128)S(1)}, f32[1,768,512]{2,1,0:T(8,128)}, u32[]{:S(2)}) %copy-start) | copy-done | bytes 1572888
  2.7 0.0 copy-start.1
  2.7 1.1 %copy-done.1 = bf16[1,768,512]{2,1,0:T(8,128)(2,1)S(1)} copy-done((bf16[1,768,512]{2,1,0:T(8,128)(2,1)S(1)}, bf16[1,768,512]{2,1,0:T(8,128)(2,1)}, u32[]{:S(2)}) %copy-start.1) | copy-done | bytes 786456
  3.8 0.0 copy-start.2
  3.8 0.8 copy-done.2
  4.6 0.0 copy-start.3
  4.6 1.0 %copy-done.3 = bf16[4,256,256]{2,1,0:T(8,128)(2,1)S(1)} copy-done((bf16[4,256,256]{2,1,0:T(8,128)(2,1)S(1)}, bf16[4,256,256]{2,1,0:T(8,128)(2,1)}, u32[]{:S(2)}) %copy-start.3) | copy-done | bytes 524312
  5.7 72.8 %shard_map.77 = (f32[768,512]{1,0:T(8,128)S(1)}, f32[768,512]{1,0:T(8,128)S(1)}) custom-call(s32[1,1]{1,0:T(1,128)} %bitcast.6.counts_ref, bf16[768,6144]{1,0:T(8,128)(2,1)} %bitcast.11, bf16[768,512]{1,0:T(8,128)(2,1)S(1)} %bitcast.9, f32[768,512]{1,0:T(8,128)S(1)} %bitcast.8, s32[12,8,128]{2,1,0:T(8,128)S(1)} %bitcast.10, bf16[4,256,256]{2,1,0:T(8,128)(2,1)S(1)} %copy-done.3), custom_call_target="tpu_custom_call" | custom-call | flops 4831838208 | bytes 9437184 | tf_op jit(solution)/shard_map/pallas_call | solution.py:415
  78.5 1.1 %copy.10 = f32[1,768,512]{2,1,0:T(8,128)} copy(f32[1,768,512]{2,1,0:T(8,128)S(1)} %bitcast.7) | data formatting | bytes 3145728
  79.6 1.1 %copy.11 = f32[768,512]{1,0:T(8,128)} copy(f32[768,512]{1,0:T(8,128)S(1)} %get-tuple-element.7) | data formatting | bytes 3145728
Async XLA Ops:
  1.3 1.4 %copy-start = (f32[1,768,512]{2,1,0:T(8,128)S(1)}, f32[1,768,512]{2,1,0:T(8,128)}, u32[]{:S(2)}) copy-start(f32[1,768,512]{2,1,0:T(8,128)} %param.8) | copy-start | bytes 4718596
  2.7 1.1 %copy-start.1 = (bf16[1,768,512]{2,1,0:T(8,128)(2,1)S(1)}, bf16[1,768,512]{2,1,0:T(8,128)(2,1)}, u32[]{:S(2)}) copy-start(bf16[1,768,512]{2,1,0:T(8,128)(2,1)} %param.7) | copy-start | bytes 2359300
  3.8 0.8 copy-start.2
  4.6 1.0 %copy-start.3 = (bf16[4,256,256]{2,1,0:T(8,128)(2,1)S(1)}, bf16[4,256,256]{2,1,0:T(8,128)(2,1)}, u32[]{:S(2)}) copy-start(bf16[4,256,256]{2,1,0:T(8,128)(2,1)} %constant.2.clone.tables) | copy-start | bytes 1572868

commit v5 on v4

--- a/solution.py
+++ b/solution.py
@@ -13,6 +13,7 @@
 CH = 64
 MESH = pl.DeviceIdType.MESH
 LEVELS = 32000.0
+DEPTH = 3
 
 
 def cosine_tables():
@@ -71,16 +72,17 @@
 
 def kernel(
     sizes,
-    counts_ref, act_hbm, grad_hbm, mom_hbm, places_ref, tables,
+    counts_ref, act_hbm, grad_hbm, mom_hbm, places_ref, tables_hbm,
     mom, directions,
     own_act, sib_act, own_grad, sib_grad, flipped, acc, coded, scales, in_coded, in_scales,
-    lists, values, mask, cols_hot, total,
+    lists, values, mask, cols_hot, total, tables,
     act_sem, sib_send, sib_recv, misc_sem, out_send, out_recv, rep_send, rep_recv,
 ):
     lines, reps, rows, chunk, pieces, width, tokens = sizes
     pairs = width // CH // 2
     tile_rows = rows // CH
     piece_tiles = chunk // CH
+    span = 2 * lists.shape[-1]
     f = lax.axis_index("fsdp")
     rep = lax.axis_index("rep")
     z, core = f // 2, f % 2
@@ -91,6 +93,7 @@
 
     grad_own = pltpu.make_async_copy(grad_hbm, own_grad, misc_sem.at[0])
     mom_own = pltpu.make_async_copy(mom_hbm, mom, misc_sem.at[1])
+    tables_own = pltpu.make_async_copy(tables_hbm, tables, misc_sem.at[4])
     grad_own.start()
 
     barrier = pltpu.get_barrier_semaphore()
@@ -242,9 +245,7 @@
         return wait
 
     def line_step(k, carry):
-        @pl.when(k >= 2)
-        def _():
-            each(k - 2, sent(0, 1), sent(1, -1))
+        each(k - DEPTH, sent(0, 1), sent(1, -1))
 
         each(k + 2, fetch, fetch)
 
@@ -268,18 +269,20 @@
         return carry
 
     def hot_step(n, carry):
-        codes = lists[n // tile_rows, n % tile_rows]
-        for pair in range(pairs):
-            cols_hot[n, pair] = column_hot(codes, pair)
+        for r in range(reps):
+            for pair in range(pairs):
+                cols_hot[n, pair, :, r * span : (r + 1) * span] = column_hot(lists[r, n], pair)
         return carry
 
     def prepare():
         mom_own.start()
+        tables_own.start()
         lax.fori_loop(0, tile_rows, mask_step, 0)
         for o in range(1, reps):
             list_copy(o).wait()
-        lax.fori_loop(0, reps * tile_rows, hot_step, 0)
+        lax.fori_loop(0, tile_rows, hot_step, 0)
         mom_own.wait()
+        tables_own.wait()
 
     middle = (z > 0) & (z < lines - 1)
 
@@ -302,7 +305,7 @@
         def tile_step(h, carry):
             i = m * piece_tiles + h
             for pair in range(pairs):
-                result = jnp.zeros((2 * CH, 2 * CH), jnp.float32)
+                parts = []
                 for r in range(reps):
                     row = row_codes(lists[r, i], pair)
                     a, b = pair_rows(values[r, i], pair)
@@ -316,7 +319,8 @@
                         ],
                         axis=0,
                     ).astype(jnp.bfloat16)
-                    result += dot(both, cols_hot[r * tile_rows + i, pair], ((1,), (1,)))
+                    parts.append(both)
+                result = dot(jnp.concatenate(parts, axis=1), cols_hot[i, pair], ((1,), (1,)))
                 total[pl.ds(pl.multiple_of(h * CH, CH), CH), 2 * CH * pair : 2 * CH * (pair + 1)] = (
                     result[:CH] + result[CH:]
                 )
@@ -350,7 +354,7 @@
             picks = []
             for pair in range(pairs):
                 at = (slice(h * CH, (h + 1) * CH), slice(2 * CH * pair, 2 * CH * (pair + 1)))
-                cols = cols_hot[rep * tile_rows + i, pair]
+                cols = cols_hot[i, pair, :, pl.ds(pl.multiple_of(rep * span, span), span)]
                 found = dot(jnp.concatenate([head[at], tail[at]], axis=0), cols)
                 found = found[:CH] + found[CH:]
                 row = row_codes(codes, pair)
@@ -388,7 +392,7 @@
         return carry
 
     lax.fori_loop(0, steps + 1, left_step, 0)
-    for k in (steps - 1, steps):
+    for k in range(steps + 1 - DEPTH, steps + 1):
         each(k, sent(0, 1), sent(1, -1))
 
 
@@ -418,7 +422,7 @@
             pltpu.VMEM((rows, width), jnp.float32),
             pltpu.VMEM((rows, width), jnp.float32),
         ),
-        in_specs=[vmem, hbm, hbm, hbm, vmem, vmem],
+        in_specs=[vmem, hbm, hbm, hbm, vmem, hbm],
         out_specs=(vmem, vmem),
         scratch_shapes=[
             pltpu.VMEM((count, tokens, chunk), jnp.bfloat16),
@@ -434,19 +438,20 @@
             pltpu.VMEM((reps, tile_rows, tile_cols, slots), jnp.int32),
             pltpu.VMEM((reps, tile_rows, tile_cols, slots), jnp.float32),
             pltpu.VMEM((rows, width), jnp.float32),
-            pltpu.VMEM((reps * tile_rows, tile_cols // 2, 2 * CH, 2 * slots), jnp.bfloat16),
+            pltpu.VMEM((tile_rows, tile_cols // 2, 2 * CH, reps * 2 * slots), jnp.bfloat16),
             pltpu.VMEM((chunk, width), jnp.float32),
+            pltpu.VMEM((4, 4 * CH, 4 * CH), jnp.bfloat16),
             dma((count,)),
             dma((count,)),
             dma((count,)),
-            dma((4,)),
+            dma((5,)),
             dma((2, count)),
             dma((2, 2, count)),
             dma((pieces + 1, reps)),
             dma((pieces + 1, reps)),
         ],
         compiler_params=pltpu.CompilerParams(
-            collective_id=0, has_side_effects=True, vmem_limit_bytes=48 * 1024 * 1024
+            collective_id=0, has_side_effects=True, vmem_limit_bytes=60 * 1024 * 1024 + 768 * 1024
         ),
         cost_estimate=pl.CostEstimate(
             flops=2 * tokens * model * width, bytes_accessed=2 * tokens * model, transcendentals=0

time: 81 us -> 76.4 us (0.943)
  local copies, waits for them, and re-layouts: 6.66 us -> 2.29 us
    unnamed x10 -> x2, local copies, waits for them, and re-layouts: 6.66 us -> 2.29 us
where the time goes in v5:
time: 76.4 us; the launch traced here: 76.2 us
  Pallas kernels  72.6 us (95%)
  local copies, waits for them, and re-layouts  2.29 us (3%)
  between operations  1.29 us (2%)
    pallas_call x1, Pallas kernels, body(): pl.pallas_call(functools.partial(kernel, sizes), out_shape=(pltpu.VMEM((r...  72.6 us
    unnamed x2, local copies, waits for them, and re-layouts  2.29 us

profile of v5, /device:TPU:8, one launch (start us, length us, event | category | flops | bytes accessed | tf_op | source)
XLA Modules:
  0.0 76.2 jit_solution(7298612403310168385)
XLA Ops:
  1.3 72.6 %shard_map.77 = (f32[768,512]{1,0:T(8,128)S(1)}, f32[768,512]{1,0:T(8,128)S(1)}) custom-call(s32[1,1]{1,0:T(1,128)} %bitcast.6.counts_ref, bf16[768,6144]{1,0:T(8,128)(2,1)} %bitcast.8, bf16[768,512]{1,0:T(8,128)(2,1)} %bitcast.10, f32[768,512]{1,0:T(8,128)} %bitcast.9, s32[12,8,128]{2,1,0:T(8,128)} %bitcast.11, bf16[4,256,256]{2,1,0:T(8,128)(2,1)} %constant.2.clone.tables_hbm), custom_call_target="tpu_custom_call" | custom-call | flops 4831838208 | bytes 9437184 | tf_op jit(solution)/shard_map/pallas_call | solution.py:419
  73.9 1.1 %copy.10 = f32[1,768,512]{2,1,0:T(8,128)} copy(f32[1,768,512]{2,1,0:T(8,128)S(1)} %bitcast.7) | data formatting | bytes 3145728
  75.1 1.1 %copy.11 = f32[768,512]{1,0:T(8,128)} copy(f32[768,512]{1,0:T(8,128)S(1)} %get-tuple-element.7) | data formatting | bytes 3145728

commit v6 on v5

--- a/solution.py
+++ b/solution.py
@@ -13,7 +13,7 @@
 CH = 64
 MESH = pl.DeviceIdType.MESH
 LEVELS = 32000.0
-DEPTH = 3
+DEPTH = 6
 
 
 def cosine_tables():
@@ -188,6 +188,7 @@
     grad_sib.wait()
     flipped[1] = sib_grad[...].T
     each(1, fetch, fetch)
+    each(2, fetch, fetch)
     for o in range(1, reps):
         list_copy(o).start()
 
@@ -247,7 +248,7 @@
     def line_step(k, carry):
         each(k - DEPTH, sent(0, 1), sent(1, -1))
 
-        each(k + 2, fetch, fetch)
+        each(k + 3, fetch, fetch)
 
         @pl.when(k < pieces)
         def _():
@@ -401,7 +402,7 @@
     tokens, model = inputs.shape
     owned, width = moment.shape
     tile_cols, slots = places.shape[1:]
-    chunk = 4 * CH
+    chunk = 2 * CH
     fill = -owned % chunk
     rows = owned + fill
     if fill:

time: 76.4 us -> 91.2 us (1.19)
  Pallas kernels: 72.6 us -> 87.4 us
    pallas_call x1, Pallas kernels: 72.6 us -> 87.4 us  [body(): pl.pallas_call(functools.partial(kernel, sizes), out_shape=(pltpu.VMEM((r...]
where the time goes in v6:
time: 91.2 us; the launch traced here: 90.9 us
  Pallas kernels  87.4 us (96%)
  local copies, waits for them, and re-layouts  2.29 us (3%)
  between operations  1.29 us (1%)
    pallas_call x1, Pallas kernels, body(): pl.pallas_call(functools.partial(kernel, sizes), out_shape=(pltpu.VMEM((r...  87.4 us
    unnamed x2, local copies, waits for them, and re-layouts  2.29 us

profile of v6, /device:TPU:8, one launch (start us, length us, event | category | flops | bytes accessed | tf_op | source)
XLA Modules:
  0.0 90.9 jit_solution(12654468992896460797)
XLA Ops:
  1.3 87.4 %shard_map.77 = (f32[768,512]{1,0:T(8,128)S(1)}, f32[768,512]{1,0:T(8,128)S(1)}) custom-call(s32[1,1]{1,0:T(1,128)} %bitcast.6.counts_ref, bf16[768,6144]{1,0:T(8,128)(2,1)} %bitcast.8, bf16[768,512]{1,0:T(8,128)(2,1)} %bitcast.10, f32[768,512]{1,0:T(8,128)} %bitcast.9, s32[12,8,128]{2,1,0:T(8,128)} %bitcast.11, bf16[4,256,256]{2,1,0:T(8,128)(2,1)} %constant.2.clone.tables_hbm), custom_call_target="tpu_custom_call" | custom-call | flops 4831838208 | bytes 9437184 | tf_op jit(solution)/shard_map/pallas_call | solution.py:420
  88.6 1.1 %copy.10 = f32[1,768,512]{2,1,0:T(8,128)} copy(f32[1,768,512]{2,1,0:T(8,128)S(1)} %bitcast.7) | data formatting | bytes 3145728
  89.8 1.1 %copy.11 = f32[768,512]{1,0:T(8,128)} copy(f32[768,512]{1,0:T(8,128)S(1)} %get-tuple-element.7) | data formatting | bytes 3145728

commit v7 on v5

--- a/solution.py
+++ b/solution.py
@@ -74,7 +74,7 @@
     sizes,
     counts_ref, act_hbm, grad_hbm, mom_hbm, places_ref, tables_hbm,
     mom, directions,
-    own_act, sib_act, own_grad, sib_grad, flipped, acc, coded, scales, in_coded, in_scales,
+    acts, own_grad, sib_grad, flipped, acc, coded, scales, in_coded, in_scales,
     lists, values, mask, cols_hot, total, tables,
     act_sem, sib_send, sib_recv, misc_sem, out_send, out_recv, rep_send, rep_recv,
 ):
@@ -121,11 +121,11 @@
         return act_hbm.at[:, pl.ds(pl.multiple_of(start, 128), chunk)]
 
     def own_copy(q):
-        return pltpu.make_async_copy(source(q, core), own_act.at[q], act_sem.at[q])
+        return pltpu.make_async_copy(source(q, core), acts.at[q, pl.ds(0, tokens)], act_sem.at[q])
 
     def sib_copy(q):
         return pltpu.make_async_remote_copy(
-            src_ref=source(q, 1 - core), dst_ref=sib_act.at[q],
+            src_ref=source(q, 1 - core), dst_ref=acts.at[q, pl.ds(tokens, tokens)],
             send_sem=sib_send.at[q], recv_sem=sib_recv.at[q],
             device_id=sibling, device_id_type=MESH,
         )
@@ -184,9 +184,9 @@
         )
 
     grad_own.wait()
-    flipped[0] = own_grad[...].T
+    flipped[:, :tokens] = own_grad[...].T
     grad_sib.wait()
-    flipped[1] = sib_grad[...].T
+    flipped[:, tokens:] = sib_grad[...].T
     each(1, fetch, fetch)
     for o in range(1, reps):
         list_copy(o).start()
@@ -194,7 +194,7 @@
     def partial(q):
         own_copy(q).wait()
         sib_copy(q).wait_recv()
-        acc[...] = dot(flipped[0], own_act[q]) + dot(flipped[1], sib_act[q])
+        acc[...] = dot(flipped[...], acts[q])
 
     def chunk_copies(q, way, step):
         return [
@@ -425,11 +425,10 @@
         in_specs=[vmem, hbm, hbm, hbm, vmem, hbm],
         out_specs=(vmem, vmem),
         scratch_shapes=[
-            pltpu.VMEM((count, tokens, chunk), jnp.bfloat16),
-            pltpu.VMEM((count, tokens, chunk), jnp.bfloat16),
+            pltpu.VMEM((count, 2 * tokens, chunk), jnp.bfloat16),
             pltpu.VMEM((tokens, width), jnp.bfloat16),
             pltpu.VMEM((tokens, width), jnp.bfloat16),
-            pltpu.VMEM((2, width, tokens), jnp.bfloat16),
+            pltpu.VMEM((width, 2 * tokens), jnp.bfloat16),
             pltpu.VMEM((width, chunk), jnp.float32),
             pltpu.VMEM((count, width, chunk), jnp.int16),
             pltpu.VMEM((count, 1, chunk), jnp.float32),

time: 76.4 us -> 76.4 us (level)
  no operation moved by 1% of the time
where the time goes in v7:
time: 76.4 us; the launch traced here: 76.2 us
  Pallas kernels  72.6 us (95%)
  local copies, waits for them, and re-layouts  2.29 us (3%)
  between operations  1.29 us (2%)
    pallas_call x1, Pallas kernels, body(): pl.pallas_call(functools.partial(kernel, sizes), out_shape=(pltpu.VMEM((r...  72.6 us
    unnamed x2, local copies, waits for them, and re-layouts  2.29 us

profile of v7, /device:TPU:8, one launch (start us, length us, event | category | flops | bytes accessed | tf_op | source)
XLA Modules:
  0.0 76.2 jit_solution(14784407072678371719)
XLA Ops:
  1.3 72.6 %shard_map.77 = (f32[768,512]{1,0:T(8,128)S(1)}, f32[768,512]{1,0:T(8,128)S(1)}) custom-call(s32[1,1]{1,0:T(1,128)} %bitcast.6.counts_ref, bf16[768,6144]{1,0:T(8,128)(2,1)} %bitcast.8, bf16[768,512]{1,0:T(8,128)(2,1)} %bitcast.10, f32[768,512]{1,0:T(8,128)} %bitcast.9, s32[12,8,128]{2,1,0:T(8,128)} %bitcast.11, bf16[4,256,256]{2,1,0:T(8,128)(2,1)} %constant.2.clone.tables_hbm), custom_call_target="tpu_custom_call" | custom-call | flops 4831838208 | bytes 9437184 | tf_op jit(solution)/shard_map/pallas_call | solution.py:419
  73.9 1.1 %copy.10 = f32[1,768,512]{2,1,0:T(8,128)} copy(f32[1,768,512]{2,1,0:T(8,128)S(1)} %bitcast.7) | data formatting | bytes 3145728
  75.1 1.1 %copy.11 = f32[768,512]{1,0:T(8,128)} copy(f32[768,512]{1,0:T(8,128)S(1)} %get-tuple-element.7) | data formatting | bytes 3145728
